TPU v7x, 768 devices: a whole 4x8x12 slice. The times are simulated.
768 devices in a mesh: img: 8 (over x, z_hi), txt: 96 (over y, z_lo, core).
Axes of the slice: x: 4, y: 8, z: 12 (z_hi: 2, z_lo: 6; z = z_hi * 6 + z_lo), core: 2. Of those that a mesh axis runs over, the one named last changes fastest.
Arguments:
- picture_vectors: bfloat16 [12288, 768], P(('img', 'txt')), may hold values from -6 to 6
- caption_vectors: bfloat16 [12288, 768], P(('txt', 'img')), may hold values from -6 to 6
- heat_exponent: float32 [], replicated, may hold values from 1.4 to 2.8
- offset_shift: float32 [], replicated, may hold values from -6 to -3
Outputs:
- grad_image: float32 [12288, 768], P(('img', 'txt'))
- grad_text: float32 [12288, 768], P(('txt', 'img'))
- couple_means: float32 [3], replicated
All inputs are finite; a program needn't handle non-finite values.
Results may differ from a plain program's by a relative error of at most 0.0033.
The roundings to bfloat16 on the way count: a program that leaves them out, or rounds other values in their place, can miss the bound.
Values may be sent and summed in bfloat16 or wider, within the bound.
A program may use at most 32 MiB of HBM per device.

v0:
```python
import jax
import jax.numpy as jnp
from jax import lax
from jax.sharding import PartitionSpec as P

epsilon = 1e-06


def normalize(raw):
    values = raw.astype(jnp.float32)
    norm_rows = jnp.sqrt(jnp.sum(values * values, axis=1, keepdims=True) + epsilon)
    return (values / norm_rows, norm_rows)


def back_norm(unit, direction, norm_rows):
    inner = jnp.sum(unit * direction, axis=1, keepdims=True)
    return (direction - unit * inner) / norm_rows


def per_device(picture_vectors, caption_vectors, heat_exponent, offset_shift):
    image_unit, image_norm = normalize(picture_vectors)
    text_unit, text_norm = normalize(caption_vectors)
    image_bf = image_unit.astype(jnp.bfloat16)
    text_bf = text_unit.astype(jnp.bfloat16)
    heat_factor = jnp.exp(heat_exponent)
    image_rows = lax.all_gather(image_bf, "txt", axis=0, tiled=True)
    text_rows = lax.all_gather(text_bf, "img", axis=0, tiled=True)
    row_first = lax.axis_index("img") * image_rows.shape[0]
    col_first = lax.axis_index("txt") * text_rows.shape[0]
    col_ids = col_first + jnp.arange(text_rows.shape[0], dtype=jnp.int32)
    cosine_table = jnp.dot(image_rows, text_rows.T, preferred_element_type=jnp.float32)
    couple_scores = heat_factor * cosine_table + offset_shift
    row_ids = row_first + jnp.arange(image_rows.shape[0], dtype=jnp.int32)
    label = jnp.where(row_ids[:, None] == col_ids[None, :], 1.0, -1.0).astype(jnp.float32)
    pair_loss = jax.nn.softplus(-label * couple_scores)
    couple_weight = -label * jax.nn.sigmoid(-label * couple_scores)
    cosine_table, pair_loss, couple_weight = (cosine_table, pair_loss, couple_weight)
    stretched_cosines = (heat_factor * couple_weight).astype(jnp.bfloat16)
    image_term = jnp.dot(stretched_cosines, text_rows, preferred_element_type=jnp.float32)
    image_dir = lax.psum_scatter(image_term, "txt", scatter_dimension=0, tiled=True)
    text_term = jnp.einsum(
        "rc,re->ce", stretched_cosines, image_rows, preferred_element_type=jnp.float32
    )
    text_dir = lax.psum_scatter(text_term, "img", scatter_dimension=0, tiled=True)
    penalty_accumulated, weight_accumulated, multiplied_accumulated = lax.psum(
        (jnp.sum(pair_loss), jnp.sum(couple_weight), jnp.sum(couple_weight * cosine_table)),
        ("img", "txt"),
    )
    sample_number = float(image_rows.shape[0] * lax.axis_size("img"))
    grad_image = back_norm(image_unit, image_dir, image_norm)
    grad_text = back_norm(text_unit, text_dir, text_norm)
    couple_means = jnp.stack(
        [penalty_accumulated, weight_accumulated, heat_factor * multiplied_accumulated]
    ) / (sample_number * sample_number)
    return (grad_image, grad_text, couple_means)


def solution(mesh):
    in_specs = (P(("img", "txt"), None), P(("txt", "img"), None), P(), P())
    out_specs = (P(("img", "txt"), None), P(("txt", "img"), None), P())
    return jax.shard_map(
        per_device, mesh=mesh, in_specs=in_specs, out_specs=out_specs, check_vma=False
    )
```

profile of v0, /device:TPU:1, one launch (start us, length us, event | category | flops | bytes accessed | tf_op | source)
XLA Modules:
  0.0 864.1 jit_solution(7074460672597010158)
XLA Ops:
  7.2 0.0 all-gather.2.cloned.1.call-start
  7.2 0.9 fusion.3
  8.1 1.4 fusion.5
  9.5 0.0 all-gather.2.cloned.1.call-update
  9.5 0.0 reduce-scatter.5.cloned.1.call-start
  10.9 0.9 fusion.4
  11.8 0.8 fusion.6
  12.6 54.5 %all_gather.7 = bf16[128,768]{1,0:T(8,128)(2,1)S(1)} all-gather(bf16[16,768]{1,0:T(8,128)(2,1)S(1)} %fusion.6), channel_id=1, replica_groups=mesh['img'=8,'txt'=96] {'img'}, dimensions={0}, use_global_device_ids=true | all-gather | bytes 221184 | tf_op jit(solution)/shard_map/all_gather | solution.py:27
  67.1 124.7 %all-gather.2.cloned.1.call-done = bf16[1536,768]{1,0:T(8,128)(2,1)} async-done(((bf16[16,768]{1,0:T(8,128)(2,1)}), bf16[1536,768]{1,0:T(8,128)(2,1)}) %all-gather.2.cloned.1.call-update) | async-done | bytes 2359312 | tf_op jit(solution)/shard_map/all_gather | solution.py:26
  191.8 0.0 copy-start.2
  191.8 3.4 fusion
  195.3 0.0 copy-done.2
  195.3 1.7 fusion.1
  196.9 0.0 reduce-scatter.5.cloned.1.call-update
  197.0 0.0 reduce-scatter.3.cloned.1.call-start
  197.0 3.1 fusion.2
  200.1 0.0 copy-start
  200.1 0.0 copy-start.1
  200.1 0.0 reduce-scatter.3.cloned.1.call-update
  200.1 109.9 %all-reduce = (f32[]{:T(128)}, f32[1]{0:T(128)}, f32[1]{0:T(128)}) all-reduce(f32[]{:T(128)} %get-tuple-element.5, f32[1]{0:T(128)} %bitcast.1, f32[1]{0:T(128)} %bitcast), channel_id=1, replica_groups=mesh['img'=8,'txt'=96] {'img','txt'}, use_global_device_ids=true, to_apply=%region_11.12 | all-reduce | flops 3 | bytes 24 | tf_op jit(solution)/shard_map/psum | solution.py:45
  310.7 1.9 maximum_multiply_fusion
  312.6 0.0 reduce-scatter.5.cloned.1.call-done
  312.6 0.0 copy-done
  312.6 1.0 multiply_reduce_fusion.1
  313.6 1.5 subtract_divide_fusion
  315.1 540.0 %reduce-scatter.3.cloned.1.call-done = f32[16,768]{1,0:T(8,128)} async-done(((f32[1536,768]{1,0:T(8,128)}), f32[16,768]{1,0:T(8,128)}) %reduce-scatter.3.cloned.1.call-update) | async-done | bytes 49168 | tf_op jit(solution)/shard_map/reduce_scatter | solution.py:40
  855.1 0.0 copy-done.1
  855.1 1.0 multiply_reduce_fusion.2
  856.1 1.5 subtract_divide_fusion.1
  (4 shorter events, 0.0 us)
Async XLA Ops:
  7.2 184.7 %all-gather.2.cloned.1.call-start = ((), (), s32[]{:S(2)}) async-start(), calls=%async_computation.2 | async-start | bytes 2383872 | tf_op jit(solution)/shard_map/all_gather | solution.py:26
  9.5 303.1 %reduce-scatter.5.cloned.1.call-start = ((), (), s32[]{:S(2)}) async-start(), calls=%async_computation.4 | async-start | bytes 442368 | tf_op jit(solution)/shard_map/reduce_scatter | solution.py:44
  191.8 3.4 copy-start.2
  197.0 658.1 %reduce-scatter.3.cloned.1.call-start = ((), (), s32[]{:S(2)}) async-start(), calls=%async_computation.3 | async-start | bytes 4767744 | tf_op jit(solution)/shard_map/reduce_scatter | solution.py:40
  200.1 112.5 %copy-start = (bf16[16,768]{1,0:T(8,128)(2,1)S(1)}, bf16[16,768]{1,0:T(8,128)(2,1)}, u32[]{:S(2)}) copy-start(bf16[16,768]{1,0:T(8,128)(2,1)} %param.5) | copy-start | bytes 73732
  200.1 655.0 %copy-start.1 = (bf16[16,768]{1,0:T(8,128)(2,1)S(1)}, bf16[16,768]{1,0:T(8,128)(2,1)}, u32[]{:S(2)}) copy-start(bf16[16,768]{1,0:T(8,128)(2,1)} %param.4) | copy-start | bytes 73732
Sparse Core Ops, SparseCore 0:
  11.1 180.7 all-gather.1
  197.1 100.2 reduce-scatter.4
  300.5 554.5 reduce-scatter.2
where the time goes:
time: 873 us; the launch traced here: 864 us
  waiting for transfers between devices  665 us (76%)
  blocking collectives  164 us (19%)
  between operations  15.8 us (2%)
  other arithmetic  10.8 us (1%)
    reduce_scatter x1, waiting for transfers between devices, per_device(): lax.psum_scatter(image_term, 'txt', scatter_dimension=0, tiled=True)  540 us
    all_gather x1, waiting for transfers between devices, per_device(): image_rows = lax.all_gather(image_bf, 'txt', axis=0, tiled=True)  125 us
    psum x1, blocking collectives, per_device(): lax.psum((jnp.sum(pair_loss), jnp.sum(couple_weight), jnp.sum(couple_weig...  110 us
    all_gather x1, blocking collectives, per_device(): text_rows = lax.all_gather(text_bf, 'img', axis=0, tiled=True)  54.5 us
  transfers between devices with their start and end apart: 3, of which 2 were waited for; matrix products, arithmetic and copies ran while one was open for 1% of the time, Pallas kernels for 0%

commit v1 on v0

v1 whole, which is shorter than its diff:
```python
import functools

import jax
import jax.numpy as jnp
from jax import lax
from jax.experimental import pallas as pl
from jax.experimental.pallas import tpu as pltpu
from jax.sharding import PartitionSpec as P

MESH = pl.DeviceIdType.MESH
NX, NY, NZ = 4, 8, 12
B, E = 16, 768
EPS = 1e-6
COUNT = 12288.0

DY = (0, 1, 7, 2, 6, 3, 5, 4)
GROUPS = ((0, 1), (1, 3), (3, 5), (5, 8))
NEAR = (0, 1, 11, 2)
IMG, TXT = NX * NY * B, NZ * 2 * B
XR, CR = NY * B, NZ * B


def kernel(
    pic, cap, heat, shift, g_img, g_txt, means,
    images, texts, sims, scaled, scaled_t, img_send, img_own, txt_send, txt_own,
    from_x, to_y, from_y, from_c, to_near, from_near, to_far, from_far, part, sum_in,
    s_gather, r_gather, s_scatter, r_scatter, s_sum, r_sum,
):
    img, txt = lax.axis_index("img"), lax.axis_index("txt")
    x, y, c = img // 2, txt // 12, txt % 2
    z = (img % 2) * 6 + (txt // 2) % 6
    way = 1 - 2 * c

    def at(dx=0, dy=0, dz=0, dc=0):
        zz = (z + way * dz + 2 * NZ) % NZ
        return (((x + dx + NX) % NX) * 2 + zz // 6,
                (((y + dy + NY) % NY) * 6 + zz % 6) * 2 + (c + dc) % 2)

    peers = [at(dx=d) for d in (1, 2, 3)] + [at(dy=d) for d in range(1, 8)]
    peers += [at(dz=d) for d in (1, 11, 2, 10, 4, 8)] + [at(dc=1)]
    entry = pltpu.get_barrier_semaphore()
    for peer in peers:
        pl.semaphore_signal(entry, inc=1, device_id=peer, device_id_type=MESH)

    def normalize(ref):
        values = ref[...].astype(jnp.float32)
        norm = jnp.sqrt(jnp.sum(values * values, axis=1, keepdims=True) + EPS)
        return values / norm, norm

    img_unit, img_norm = normalize(pic)
    txt_unit, txt_norm = normalize(cap)
    images[0:B, :] = img_unit.astype(jnp.bfloat16)
    texts[0:B, :] = txt_unit.astype(jnp.bfloat16)
    pl.semaphore_wait(entry, len(peers))

    sends = []

    def sender(ssem, rsem):
        used = [0]

        def send(src, dst, device):
            i = used[0]
            used[0] += 1
            copy = pltpu.make_async_remote_copy(
                src_ref=src, dst_ref=dst, send_sem=ssem.at[i], recv_sem=rsem.at[i],
                device_id=device, device_id_type=MESH)
            copy.start()
            sends.append(copy)
            return copy

        return send

    def rows(ref, first, count):
        return ref.at[pl.ds(first, count)]

    send = sender(s_gather, r_gather)
    own_t, own_i = rows(texts, 0, B), rows(images, 0, B)
    far = [send(own_t, rows(texts, f * B, B), at(dz=-4 * f)) for f in (1, 2)]
    over_y = {k: send(own_i, rows(images, k * B, B), at(dy=-DY[k])) for k in range(7, 0, -1)}
    arrive_x, arrive_z, arrive_c = [], [], []

    def forward_x(g):
        a, b = GROUPS[g]
        for dx in (2, 1, 3):
            arrive_x.append(send(rows(images, a * B, (b - a) * B),
                                 rows(images, dx * XR + a * B, (b - a) * B), at(dx=-dx)))

    forward_x(0)
    near = {n: [send(own_t, rows(texts, n * 3 * B, B), at(dz=-NEAR[n]))] for n in (3, 1, 2)}
    for g in (1, 2):
        for k in range(*GROUPS[g]):
            over_y[k].wait_recv()
        forward_x(g)
    for copy in far:
        copy.wait_recv()
    for n in (3, 1, 2):
        near[n].append(send(rows(texts, B, 2 * B), rows(texts, (n * 3 + 1) * B, 2 * B), at(dz=-NEAR[n])))
    arrive_c.append(send(rows(texts, 0, 3 * B), rows(texts, CR, 3 * B), at(dc=1)))
    for k in range(*GROUPS[3]):
        over_y[k].wait_recv()
    forward_x(3)
    for n in (1, 2, 3):
        for copy in near[n]:
            copy.wait_recv()
        arrive_c.append(send(rows(texts, n * 3 * B, 3 * B), rows(texts, CR + n * 3 * B, 3 * B), at(dc=1)))
    for copy in arrive_c + arrive_x:
        copy.wait_recv()

    nt = (((1,), (1,)), ((), ()))
    sims[...] = lax.dot_general(images[...], texts[...], nt, preferred_element_type=jnp.float32)

    slot = lax.broadcasted_iota(jnp.int32, (1, TXT), 1)
    row = slot & (B - 1)
    slot = slot >> 4
    dc = jnp.where(slot >= 12, 1, 0)
    slot = slot - 12 * dc
    n = jnp.where(slot >= 9, 3, jnp.where(slot >= 6, 2, jnp.where(slot >= 3, 1, 0)))
    f = slot - 3 * n
    dz = jnp.where(n == 2, 11, jnp.where(n == 3, 2, n)) + 4 * f
    dz = jnp.where(dz >= 12, dz - 12, dz)
    zz = z + way * (1 - 2 * dc) * dz
    zz = jnp.where(zz >= 12, zz - 12, jnp.where(zz < 0, zz + 12, zz))
    z_hi = jnp.where(zz >= 6, 1, 0)
    cc = c + dc - 2 * c * dc
    txt_id = (((y * 6 + zz - 6 * z_hi) * 2 + cc) * 8 + x * 2 + z_hi) * B + row

    temp = jnp.exp(jnp.full((1, TXT), heat[0], jnp.float32))
    bias = shift[0]
    step = 32

    def pairs(i, sums):
        first = pl.multiple_of(i * step, step)
        sim = sims[pl.ds(first, step), :]
        r = lax.broadcasted_iota(jnp.int32, (step, 1), 0) + first
        s = r >> 4
        k = s & 7
        dy = jnp.where((k & 1) == 1, (k + 1) >> 1, (8 - (k >> 1)) & 7)
        xo, yo = (x + (s >> 3)) & 3, (y + dy) & 7
        img_id = ((xo * 2 + z // 6) * 96 + (yo * 6 + z % 6) * 2 + c) * B + (r & (B - 1))
        same = img_id == txt_id
        logits = temp * sim + bias
        arg = jnp.where(same, -logits, logits)
        e = jnp.exp(-jnp.abs(arg))
        loss = jnp.maximum(arg, 0.0) + jnp.log1p(e)
        sig = jnp.where(arg >= 0, 1.0, e) / (1.0 + e)
        coeff = jnp.where(same, -sig, sig)
        scaled[pl.ds(first, step), :] = (temp * coeff).astype(jnp.bfloat16)

        def fold(v):
            return jnp.sum(v.reshape(step // 8, 8, TXT), axis=0)

        return sums[0] + fold(loss), sums[1] + fold(coeff), sums[2] + fold(coeff * sim)

    zero = jnp.zeros((8, TXT), jnp.float32)
    sums = lax.fori_loop(0, IMG // step, pairs, (zero, zero, zero))

    def lanes(v):
        v = v[:, 0:128] + v[:, 128:256] + v[:, 256:384]
        return jnp.sum(v, axis=0, keepdims=True)

    sub = lax.broadcasted_iota(jnp.int32, (8, 128), 0)
    total = jnp.where(sub == 0, lanes(sums[0]), 0.0) + jnp.where(sub == 1, lanes(sums[1]), 0.0)
    total = total + jnp.where(sub == 2, lanes(sums[2]), 0.0)

    send_sum = sender(s_sum, r_sum)
    used = [0]

    def spread(stage, devices):
        copies = []
        for device in devices:
            copies.append((send_sum(part.at[stage], sum_in.at[used[0]], device), used[0]))
            used[0] += 1
        return copies

    def collect(value, copies):
        for copy, i in copies:
            copy.wait_recv()
            value = value + sum_in[i]
        return value

    part[0] = total
    sum_c = spread(0, [at(dc=1)])

    send = sender(s_scatter, r_scatter)
    scaled_t[...] = scaled[...].T
    for half in (1, 0):
        term = jnp.dot(scaled_t[half * CR:(half + 1) * CR, :], images[...], preferred_element_type=jnp.float32)
        if half:
            txt_send[...] = term.astype(jnp.bfloat16)
            over_c = send(txt_send, from_c, at(dc=1))
        else:
            txt_own[...] = term
    for dx in (2, 1, 3, 0):
        term = jnp.dot(scaled[dx * XR:(dx + 1) * XR, :], texts[...], preferred_element_type=jnp.float32)
        if dx:
            img_send[(dx - 1) * XR:dx * XR, :] = term.astype(jnp.bfloat16)
        else:
            img_own[...] = term
    over_x = {}
    for g in (3, 2, 1, 0):
        a, b = GROUPS[g]
        for dx in (2, 1, 3):
            first = (dx - 1) * XR + a * B
            over_x[g, dx] = send(rows(img_send, first, (b - a) * B), rows(from_x, first, (b - a) * B), at(dx=dx))

    total = collect(total, sum_c)
    part[1] = total
    sum_f = spread(1, [at(dz=4), at(dz=8)])

    over_c.wait_recv()
    to_near[...] = (txt_own[3 * B:, :] + from_c[3 * B:, :].astype(jnp.float32)).astype(jnp.bfloat16)
    over_near = [send(rows(to_near, (n - 1) * 3 * B, 3 * B), rows(from_near, (n - 1) * 3 * B, 3 * B), at(dz=NEAR[n]))
                 for n in (3, 1, 2)]
    txt_three = txt_own[0:3 * B, :] + from_c[0:3 * B, :].astype(jnp.float32)

    over_y = []
    for g in (3, 2, 1, 0):
        a, b = GROUPS[g]
        mine = img_own[a * B:b * B, :]
        for dx in (2, 1, 3):
            over_x[g, dx].wait_recv()
        for dx in (1, 2, 3):
            mine = mine + from_x[(dx - 1) * XR + a * B:(dx - 1) * XR + b * B, :].astype(jnp.float32)
        if g:
            to_y[(a - 1) * B:(b - 1) * B, :] = mine.astype(jnp.bfloat16)
            for k in range(b - 1, a - 1, -1):
                over_y.append(send(rows(to_y, (k - 1) * B, B), rows(from_y, (k - 1) * B, B), at(dy=DY[k])))
        else:
            img_dir = mine
        if g == 3:
            total = collect(total, sum_f)
            part[2] = total
            sum_n = spread(2, [at(dz=NEAR[n]) for n in (3, 1, 2)])
        if g == 2:
            for copy in over_near:
                copy.wait_recv()
            for n in (1, 2, 3):
                txt_three = txt_three + from_near[(n - 1) * 3 * B:n * 3 * B, :].astype(jnp.float32)
            to_far[...] = txt_three[B:, :].astype(jnp.bfloat16)
            over_far = [send(rows(to_far, (f - 1) * B, B), rows(from_far, (f - 1) * B, B), at(dz=4 * f)) for f in (1, 2)]
            txt_dir = txt_three[0:B, :]
            total = collect(total, sum_n)
            part[3] = total
            sum_x = spread(3, [at(dx=d) for d in (2, 1, 3)])

    total = collect(total, sum_x)
    part[4] = total
    sum_y = spread(4, [at(dy=d) for d in DY[:0:-1]])

    def back_norm(unit, direction, norm):
        inner = jnp.sum(unit * direction, axis=1, keepdims=True)
        return (direction - unit * inner) / norm

    for copy in over_far:
        copy.wait_recv()
    for f in (1, 2):
        txt_dir = txt_dir + from_far[(f - 1) * B:f * B, :].astype(jnp.float32)
    g_txt[...] = back_norm(txt_unit, txt_dir, txt_norm)
    for copy in over_y:
        copy.wait_recv()
    for k in range(1, 8):
        img_dir = img_dir + from_y[(k - 1) * B:k * B, :].astype(jnp.float32)
    g_img[...] = back_norm(img_unit, img_dir, img_norm)
    total = collect(total, sum_y)
    scale = 1.0 / (COUNT * COUNT)
    means[0] = jnp.sum(jnp.where(sub == 0, total, 0.0)) * scale
    means[1] = jnp.sum(jnp.where(sub == 1, total, 0.0)) * scale
    means[2] = jnp.sum(jnp.where(sub == 2, total * temp[:, 0:128], 0.0)) * scale
    for copy in sends:
        copy.wait_send()


def per_device(pictures, captions, heat, shift):
    f32, bf16 = jnp.float32, jnp.bfloat16
    vmem, smem = pl.BlockSpec(memory_space=pltpu.VMEM), pl.BlockSpec(memory_space=pltpu.SMEM)
    dma = pltpu.SemaphoreType.DMA
    return pl.pallas_call(
        kernel,
        out_shape=(
            jax.ShapeDtypeStruct((B, E), f32),
            jax.ShapeDtypeStruct((B, E), f32),
            jax.ShapeDtypeStruct((3,), f32),
        ),
        in_specs=[vmem, vmem, smem, smem],
        out_specs=(vmem, vmem, smem),
        scratch_shapes=[
            pltpu.VMEM((IMG, E), bf16),
            pltpu.VMEM((TXT, E), bf16),
            pltpu.VMEM((IMG, TXT), f32),
            pltpu.VMEM((IMG, TXT), bf16),
            pltpu.VMEM((TXT, IMG), bf16),
            pltpu.VMEM((3 * XR, E), bf16),
            pltpu.VMEM((XR, E), f32),
            pltpu.VMEM((CR, E), bf16),
            pltpu.VMEM((CR, E), f32),
            pltpu.VMEM((3 * XR, E), bf16),
            pltpu.VMEM((7 * B, E), bf16),
            pltpu.VMEM((7 * B, E), bf16),
            pltpu.VMEM((CR, E), bf16),
            pltpu.VMEM((9 * B, E), bf16),
            pltpu.VMEM((9 * B, E), bf16),
            pltpu.VMEM((2 * B, E), bf16),
            pltpu.VMEM((2 * B, E), bf16),
            pltpu.VMEM((5, 8, 128), f32),
            pltpu.VMEM((16, 8, 128), f32),
            dma((31,)), dma((31,)), dma((25,)), dma((25,)), dma((16,)), dma((16,)),
        ],
        compiler_params=pltpu.CompilerParams(
            collective_id=0, has_side_effects=True, vmem_limit_bytes=48 * 1024 * 1024),
        cost_estimate=pl.CostEstimate(flops=910_000_000, bytes_accessed=150_000, transcendentals=600_000),
        name="pairs",
    )(pictures, captions, heat.reshape(1), shift.reshape(1))


def solution(mesh):
    in_specs = (P(("img", "txt"), None), P(("txt", "img"), None), P(), P())
    out_specs = (P(("img", "txt"), None), P(("txt", "img"), None), P())
    return jax.shard_map(
        per_device, mesh=mesh, in_specs=in_specs, out_specs=out_specs, check_vma=False
    )
```

time: 873 us -> 60.7 us (0.07)
  the two profiles are of different devices: /device:TPU:1 before, /device:TPU:8 now
where the time goes in v1:
time: 60.7 us; the launch traced here: 60.4 us
  Pallas kernels  55.2 us (91%)
  local copies, waits for them, and re-layouts  3.22 us (5%)
  between operations  1.94 us (3%)
    pallas_call x1, Pallas kernels, per_device(): pl.pallas_call(kernel, out_shape=(jax.ShapeDtypeStruct((B, E), f32), jax....  55.2 us
    unnamed x7, local copies, waits for them, and re-layouts  3.22 us

profile of v1, /device:TPU:8, one launch (start us, length us, event | category | flops | bytes accessed | tf_op | source)
XLA Modules:
  0.0 60.4 jit_solution(18061481418424519582)
XLA Ops:
  1.9 0.0 copy-start
  1.9 0.7 %copy-done = bf16[16,768]{1,0:T(8,128)(2,1)S(1)} copy-done((bf16[16,768]{1,0:T(8,128)(2,1)S(1)}, bf16[16,768]{1,0:T(8,128)(2,1)}, u32[]{:S(2)}) %copy-start) | copy-done | bytes 24600
  2.7 0.0 copy-start.1
  2.7 0.7 %copy-done.1 = bf16[16,768]{1,0:T(8,128)(2,1)S(1)} copy-done((bf16[16,768]{1,0:T(8,128)(2,1)S(1)}, bf16[16,768]{1,0:T(8,128)(2,1)}, u32[]{:S(2)}) %copy-start.1) | copy-done | bytes 24600
  3.4 55.2 %pairs.1 = (f32[16,768]{1,0:T(8,128)S(1)}, f32[16,768]{1,0:T(8,128)S(1)}, f32[3]{0:T(128)S(1)}) custom-call(bf16[16,768]{1,0:T(8,128)(2,1)S(1)} %copy-done, bf16[16,768]{1,0:T(8,128)(2,1)S(1)} %copy-done.1, f32[1]{0:T(128)} %bitcast.2.heat, f32[1]{0:T(128)} %bitcast.3.shift), custom_call_target="tpu_custom_call" | custom-call | flops 910000000 | bytes 150000 | tf_op jit(solution)/shard_map/pairs/pallas_call | solution.py:277
  58.6 0.6 %copy.12 = f32[16,768]{1,0:T(8,128)} copy(f32[16,768]{1,0:T(8,128)S(1)} %get-tuple-element.6) | data formatting | bytes 98304
  59.3 0.6 %copy.13 = f32[16,768]{1,0:T(8,128)} copy(f32[16,768]{1,0:T(8,128)S(1)} %get-tuple-element.7) | data formatting | bytes 98304
  59.9 0.5 copy.14
Async XLA Ops:
  1.9 0.7 %copy-start = (bf16[16,768]{1,0:T(8,128)(2,1)S(1)}, bf16[16,768]{1,0:T(8,128)(2,1)}, u32[]{:S(2)}) copy-start(bf16[16,768]{1,0:T(8,128)(2,1)} %pic.1) | copy-start | bytes 73732
  2.7 0.7 %copy-start.1 = (bf16[16,768]{1,0:T(8,128)(2,1)S(1)}, bf16[16,768]{1,0:T(8,128)(2,1)}, u32[]{:S(2)}) copy-start(bf16[16,768]{1,0:T(8,128)(2,1)} %cap.1) | copy-start | bytes 73732

commit v2 on v0

v2 whole, which is shorter than its diff:
```python
import jax
import jax.numpy as jnp
from jax import lax
from jax.experimental import pallas as pl
from jax.experimental.pallas import tpu as pltpu
from jax.sharding import PartitionSpec as P

MESH = pl.DeviceIdType.MESH
NX, NY, NZ = 4, 8, 12
B, E = 16, 768
EPS = 1e-6
COUNT = 12288.0
HALF = E // 2

DY = (0, 1, 7, 2, 6, 3, 5, 4)
DZ = (0, 1, 11, 2, 10, 3, 9, 4, 8, 5, 7, 6)
SLOT = {d: k for k, d in enumerate(DZ)}
IMG, TXT = NX * NY * B, NZ * 2 * B
CR = NZ * B
FIRST = 5 * NX * B
PARTS = ((0, FIRST), (FIRST, IMG))
DX = (2, 1, 3)


def kernel(
    pic_in, cap_in, heat, shift, g_img, g_txt, means,
    pic, cap, images, texts, sims, scaled, scaled_t, img_term, img_send, txt_send, txt_own,
    from_x, to_y, from_y, from_c, to_z, from_z, to_far, part, sum_in,
    s_in, s_gather, r_gather, s_scatter, r_scatter, s_sum, r_sum,
):
    img, txt = lax.axis_index("img"), lax.axis_index("txt")
    x, y, c = img // 2, txt // 12, txt % 2
    z = (img % 2) * 6 + (txt // 2) % 6

    def at(dx=0, dy=0, dz=0, dc=0):
        zz = (z + dz) % NZ
        return (((x + dx) % NX) * 2 + zz // 6, (((y + dy) % NY) * 6 + zz % 6) * 2 + (c + dc) % 2)

    peers = [at(dy=d) for d in (4, 3, 5, 2, 6, 1, 7)] + [at(dx=d) for d in DX]
    peers += [at(dz=d) for d in (4, 8, 3, 9, 2, 10, 1, 11)] + [at(dc=1)]
    entry = pltpu.get_barrier_semaphore()
    for peer in peers:
        pl.semaphore_signal(entry, inc=1, device_id=peer, device_id_type=MESH)
    loads = [pltpu.make_async_copy(pic_in, pic, s_in.at[0]), pltpu.make_async_copy(cap_in, cap, s_in.at[1])]
    for load in loads:
        load.start()
    for load in loads:
        load.wait()

    def normalize(ref):
        values = ref[...].astype(jnp.float32)
        norm = jnp.sqrt(jnp.sum(values * values, axis=1, keepdims=True) + EPS)
        return values / norm, norm

    img_unit, img_norm = normalize(pic)
    txt_unit, txt_norm = normalize(cap)
    images[0:B, :] = img_unit.astype(jnp.bfloat16)
    texts[0:B, :] = txt_unit.astype(jnp.bfloat16)
    pl.semaphore_wait(entry, len(peers))

    sends = []

    def sender(ssem, rsem):
        used = [0]

        def send(src, dst, device):
            i = used[0]
            used[0] += 1
            copy = pltpu.make_async_remote_copy(
                src_ref=src, dst_ref=dst, send_sem=ssem.at[i], recv_sem=rsem.at[i],
                device_id=device, device_id_type=MESH)
            copy.start()
            sends.append(copy)
            return copy

        return send

    def slots(ref, first, count=1):
        return ref.at[pl.ds(first * B, count * B)]

    def wait(copies):
        for copy in copies:
            copy.wait_recv()

    send = sender(s_gather, r_gather)
    own_t, own_i = slots(texts, 0), slots(images, 0)
    over_z = {d: send(own_t, slots(texts, SLOT[d]), at(dz=-d)) for d in (4, 8, 3, 9, 2, 10, 1, 11)}
    over_y = {k: send(own_i, slots(images, 4 * k), at(dy=-DY[k])) for k in range(1, 8)}
    over_x, over_c = {}, []

    def forward_x(*ks):
        for k in ks:
            if k:
                over_y[k].wait_recv()
            over_x[k] = [send(slots(images, 4 * k), slots(images, 4 * k + dx), at(dx=-dx)) for dx in DX]

    def forward_c(*ds):
        first = min(SLOT[d] for d in ds)
        over_c.append(send(slots(texts, first, len(ds)), slots(texts, NZ + first, len(ds)), at(dc=1)))

    forward_x(0)
    forward_c(0)
    wait([over_z[4], over_z[8]])
    six = SLOT[6] * B
    late = [
        send(texts.at[pl.ds(SLOT[4] * B, B), pl.ds(0, HALF)], texts.at[pl.ds(six, B), pl.ds(0, HALF)], at(dz=-2)),
        send(texts.at[pl.ds(SLOT[8] * B, B), pl.ds(HALF, HALF)], texts.at[pl.ds(six, B), pl.ds(HALF, HALF)], at(dz=2)),
        send(slots(texts, SLOT[4]), slots(texts, SLOT[5]), at(dz=-1)),
        send(slots(texts, SLOT[8]), slots(texts, SLOT[7]), at(dz=1)),
    ]
    forward_x(1, 2, 3, 4)
    forward_c(4, 8)
    wait([over_z[d] for d in (1, 11, 2, 10)])
    forward_c(1, 11, 2, 10)
    forward_x(5, 6, 7)
    wait([over_z[d] for d in (3, 9)])
    forward_c(3, 9)
    wait(late)
    forward_c(5, 7, 6)

    def owner_offset(k, n):
        return jnp.where((k & 1) == 1, (k + 1) >> 1, jnp.where(k == 0, 0, n - (k >> 1)))

    col = lax.broadcasted_iota(jnp.int32, (1, TXT), 1)
    k = col >> 4
    dc = jnp.where(k >= NZ, 1, 0)
    zz = z + owner_offset(k - NZ * dc, NZ)
    zz = jnp.where(zz >= NZ, zz - NZ, zz)
    z_hi = jnp.where(zz >= 6, 1, 0)
    cc = c + dc - 2 * c * dc
    txt_id = (((y * 6 + zz - 6 * z_hi) * 2 + cc) * 8 + x * 2 + z_hi) * B + (col & (B - 1))
    temp = jnp.exp(jnp.full((1, TXT), heat[0], jnp.float32))
    bias = shift[0]
    step = 32

    def pairs(i, sums):
        first = pl.multiple_of(i * step, step)
        sim = sims[pl.ds(first, step), :]
        r = lax.broadcasted_iota(jnp.int32, (step, 1), 0) + first
        xo = (x + (r >> 4)) & (NX - 1)
        yo = (y + owner_offset(r >> 6, NY)) & (NY - 1)
        img_id = ((xo * 2 + z // 6) * 96 + (yo * 6 + z % 6) * 2 + c) * B + (r & (B - 1))
        same = img_id == txt_id
        logits = temp * sim + bias
        arg = jnp.where(same, -logits, logits)
        e = jnp.exp(-jnp.abs(arg))
        loss = jnp.maximum(arg, 0.0) + jnp.log1p(e)
        sig = jnp.where(arg >= 0, 1.0, e) / (1.0 + e)
        coeff = jnp.where(same, -sig, sig)
        scaled[pl.ds(first, step), :] = (temp * coeff).astype(jnp.bfloat16)

        def fold(v):
            return jnp.sum(v.reshape(step // 8, 8, TXT), axis=0)

        return sums[0] + fold(loss), sums[1] + fold(coeff), sums[2] + fold(coeff * sim)

    zero = jnp.zeros((8, TXT), jnp.float32)
    sums = (zero, zero, zero)
    send = sender(s_scatter, r_scatter)
    nt = (((1,), (1,)), ((), ()))
    back_x = {}
    wait(over_c)
    for p, (a, b) in enumerate(PARTS):
        ks = (range(0, 5), range(5, 8))[p]
        for k in ks:
            wait(over_x[k])
        sims[a:b, :] = lax.dot_general(images[a:b, :], texts[...], nt, preferred_element_type=jnp.float32)
        sums = lax.fori_loop(a // step, b // step, pairs, sums)
        if p:
            def whole(v):
                v = v[:, 0:128] + v[:, 128:256] + v[:, 256:384]
                return jnp.sum(jnp.sum(v, axis=0, keepdims=True), axis=1, keepdims=True)

            lane = lax.broadcasted_iota(jnp.int32, (1, 128), 1)
            total = jnp.where(lane == 0, whole(sums[0]), jnp.where(lane == 1, whole(sums[1]), whole(sums[2])))
            send_sum = sender(s_sum, r_sum)
            used = [0]

            def spread(stage, value, devices):
                part[stage] = value
                copies = []
                for device in devices:
                    copies.append((send_sum(part.at[stage], sum_in.at[used[0]], device), used[0]))
                    used[0] += 1
                return copies

            def collect(value, copies):
                for copy, i in copies:
                    copy.wait_recv()
                    value = value + sum_in[i]
                return value

            sum_c = spread(0, total, [at(dc=1)])
        term = jnp.dot(scaled[a:b, :], texts[...], preferred_element_type=jnp.float32)
        img_term[a:b, :] = term
        img_send[a:b, :] = term.astype(jnp.bfloat16)
    def send_x(*ks):
        for k in ks:
            back_x[k] = [send(slots(img_send, 4 * k + dx), slots(from_x, 4 * k + dx), at(dx=dx)) for dx in DX]

    send_x(7, 6, 5)
    scaled_t[...] = scaled[...].T
    txt_send[...] = jnp.dot(scaled_t[CR:, :], images[...], preferred_element_type=jnp.float32).astype(jnp.bfloat16)
    back_c = send(txt_send, from_c, at(dc=1))
    txt_own[...] = jnp.dot(scaled_t[0:CR, :], images[...], preferred_element_type=jnp.float32)
    total = collect(total, sum_c)
    plane = [at(dx, dy) for dy in DY[::-1] for dx in (2, 1, 3, 0) if dx or dy]
    sum_p = spread(1, total, plane)

    back_c.wait_recv()
    txt_own[...] = txt_own[...] + from_c[...].astype(jnp.float32)
    to_z[...] = txt_own[...].astype(jnp.bfloat16)
    relay = [
        send(to_z.at[pl.ds(six, B), pl.ds(0, HALF)], from_z.at[pl.ds(six, B), pl.ds(0, HALF)], at(dz=2)),
        send(to_z.at[pl.ds(six, B), pl.ds(HALF, HALF)], from_z.at[pl.ds(six, B), pl.ds(HALF, HALF)], at(dz=-2)),
        send(slots(to_z, SLOT[5]), slots(from_z, SLOT[5]), at(dz=1)),
        send(slots(to_z, SLOT[7]), slots(from_z, SLOT[7]), at(dz=-1)),
    ]
    back_z = {d: send(slots(to_z, SLOT[d]), slots(from_z, SLOT[d]), at(dz=d)) for d in (3, 9, 2, 10, 1, 11)}
    for k in (7, 6, 5):
        for copy in back_x[k]:
            copy.wait_send()
    send_x(4, 3, 2, 1, 0)

    wait(relay)

    def piece(ref, d):
        return ref[SLOT[d] * B:(SLOT[d] + 1) * B, :].astype(jnp.float32)

    side = lax.broadcasted_iota(jnp.int32, (B, E), 1) < HALF
    both = piece(from_z, 6)
    to_far[0:B, :] = (piece(txt_own, 4) + piece(from_z, 5) + jnp.where(side, both, 0.0)).astype(jnp.bfloat16)
    to_far[B:, :] = (piece(txt_own, 8) + piece(from_z, 7) + jnp.where(side, 0.0, both)).astype(jnp.bfloat16)
    for i, d in enumerate((4, 8)):
        back_z[d] = send(slots(to_far, i), slots(from_z, SLOT[d]), at(dz=d))
    back_y = []

    def image_sum(k):
        wait(back_x[k])
        first = 4 * k * B
        value = img_term[first:first + B, :]
        for dx in (1, 2, 3):
            value = value + from_x[first + dx * B:first + (dx + 1) * B, :].astype(jnp.float32)
        return value

    def send_y(*ks):
        for k in ks:
            to_y[(k - 1) * B:k * B, :] = image_sum(k).astype(jnp.bfloat16)
            back_y.append(send(slots(to_y, k - 1), slots(from_y, k - 1), at(dy=DY[k])))

    total = collect(total, sum_p)
    sum_z = spread(2, total, [at(dz=d) for d in DZ[:0:-1]])
    send_y(7, 6, 5)
    send_y(4, 3, 2, 1)
    img_dir = image_sum(0)

    def back_norm(unit, direction, norm):
        inner = jnp.sum(unit * direction, axis=1, keepdims=True)
        return (direction - unit * inner) / norm

    txt_dir = piece(txt_own, 0)
    for d in (1, 11, 2, 10, 3, 9, 4, 8):
        back_z[d].wait_recv()
        txt_dir = txt_dir + piece(from_z, d)
    g_txt[...] = back_norm(txt_unit, txt_dir, txt_norm)
    wait(back_y)
    for k in range(1, 8):
        img_dir = img_dir + from_y[(k - 1) * B:k * B, :].astype(jnp.float32)
    g_img[...] = back_norm(img_unit, img_dir, img_norm)
    total = collect(total, sum_z)
    means[...] = total * jnp.where(lane == 2, temp[:, 0:128], 1.0) * (1.0 / (COUNT * COUNT))
    early = {id(copy) for k in (7, 6, 5) for copy in back_x[k]}
    for copy in sends:
        if id(copy) not in early:
            copy.wait_send()


def hand_over(a, b, c, a_out, b_out, c_out):
    a_out[...] = a[...]
    b_out[...] = b[...]
    for i in range(3):
        c_out[i] = jnp.sum(c[:, i:i + 1])


def per_device(pictures, captions, heat, shift):
    f32, bf16 = jnp.float32, jnp.bfloat16
    hbm, vmem, smem = (pl.BlockSpec(memory_space=m) for m in (pltpu.HBM, pltpu.VMEM, pltpu.SMEM))
    dma = pltpu.SemaphoreType.DMA
    results_shape = (
        jax.ShapeDtypeStruct((B, E), f32),
        jax.ShapeDtypeStruct((B, E), f32),
        jax.ShapeDtypeStruct((1, 128), f32),
    )
    results = pl.pallas_call(
        kernel,
        out_shape=results_shape,
        in_specs=[hbm, hbm, smem, smem],
        out_specs=(vmem, vmem, vmem),
        scratch_shapes=[
            pltpu.VMEM((B, E), bf16),
            pltpu.VMEM((B, E), bf16),
            pltpu.VMEM((IMG, E), bf16),
            pltpu.VMEM((TXT, E), bf16),
            pltpu.VMEM((IMG, TXT), f32),
            pltpu.VMEM((IMG, TXT), bf16),
            pltpu.VMEM((TXT, IMG), bf16),
            pltpu.VMEM((IMG, E), f32),
            pltpu.VMEM((IMG, E), bf16),
            pltpu.VMEM((CR, E), bf16),
            pltpu.VMEM((CR, E), f32),
            pltpu.VMEM((IMG, E), bf16),
            pltpu.VMEM((7 * B, E), bf16),
            pltpu.VMEM((7 * B, E), bf16),
            pltpu.VMEM((CR, E), bf16),
            pltpu.VMEM((CR, E), bf16),
            pltpu.VMEM((CR, E), bf16),
            pltpu.VMEM((2 * B, E), bf16),
            pltpu.VMEM((3, 1, 128), f32),
            pltpu.VMEM((43, 1, 128), f32),
            dma((2,)), dma((48,)), dma((48,)), dma((44,)), dma((44,)), dma((43,)), dma((43,)),
        ],
        compiler_params=pltpu.CompilerParams(
            collective_id=0, has_side_effects=True, vmem_limit_bytes=62 * 1024 * 1024),
        cost_estimate=pl.CostEstimate(flops=910_000_000, bytes_accessed=150_000, transcendentals=600_000),
        name="pairs",
    )(pictures, captions, heat.reshape(1), shift.reshape(1))
    return pl.pallas_call(
        hand_over,
        out_shape=(*results_shape[:2], jax.ShapeDtypeStruct((3,), f32)),
        in_specs=[vmem] * 3,
        out_specs=(vmem, vmem, smem),
        compiler_params=pltpu.CompilerParams(vmem_limit_bytes=62 * 1024 * 1024),
        name="hand_over",
    )(*results)


def solution(mesh):
    in_specs = (P(("img", "txt"), None), P(("txt", "img"), None), P(), P())
    out_specs = (P(("img", "txt"), None), P(("txt", "img"), None), P())
    return jax.shard_map(
        per_device, mesh=mesh, in_specs=in_specs, out_specs=out_specs, check_vma=False
    )
```

time: 873 us -> 55.1 us (0.06)
  waiting for transfers between devices: 665 us -> 0 us
  blocking collectives: 164 us -> 0 us
  Pallas kernels: 0 us -> 52.9 us
  between operations: 15.8 us -> 1.93 us
  other arithmetic: 10.8 us -> 0 us
    reduce_scatter x2 -> x0, waiting for transfers between devices: 540 us -> none  [the longest x1 540 us: per_device(): lax.psum_scatter(image_term, 'txt', scatter_dimension=0, tiled=True)]
    all_gather x1 -> x0, waiting for transfers between devices: 125 us -> none  [per_device(): image_rows = lax.all_gather(image_bf, 'txt', axis=0, tiled=True)]
    psum x1 -> x0, blocking collectives: 110 us -> none  [per_device(): lax.psum((jnp.sum(pair_loss), jnp.sum(couple_weight), jnp.sum(couple_weig...]
    all_gather x1 -> x0, blocking collectives: 54.5 us -> none  [per_device(): text_rows = lax.all_gather(text_bf, 'img', axis=0, tiled=True)]
    pallas_call x0 -> x2, Pallas kernels: none -> 52.9 us  [the longest x1 51.4 us: per_device(): pl.pallas_call(kernel, out_shape=results_shape, in_specs=[hbm, hbm, smem,...]
  transfers between devices with their start and end apart: 3 -> 0, of which waited for: 2 -> 0; matrix products, arithmetic and copies ran while one was open for 1% -> 0% of each run, Pallas kernels for 0% -> 0%
where the time goes in v2:
time: 55.1 us; the launch traced here: 54.8 us
  Pallas kernels  52.9 us (96%)
  between operations  1.93 us (4%)
    pallas_call x1, Pallas kernels, per_device(): pl.pallas_call(kernel, out_shape=results_shape, in_specs=[hbm, hbm, smem,...  51.4 us
    pallas_call x1, Pallas kernels, per_device(): pl.pallas_call(hand_over, out_shape=(*results_shape[:2], jax.ShapeDtypeSt...  1.48 us

profile of v2, /device:TPU:1, one launch (start us, length us, event | category | flops | bytes accessed | tf_op | source)
XLA Modules:
  0.0 54.8 jit_solution(978299766808244705)
XLA Ops:
  1.9 51.4 %pairs.1 = (f32[16,768]{1,0:T(8,128)}, f32[16,768]{1,0:T(8,128)}, f32[1,128]{1,0:T(1,128)}) custom-call(bf16[16,768]{1,0:T(8,128)(2,1)} %pic_in.1, bf16[16,768]{1,0:T(8,128)(2,1)} %cap_in.1, f32[1]{0:T(128)} %bitcast.2.heat, f32[1]{0:T(128)} %bitcast.3.shift), custom_call_target="tpu_custom_call" | custom-call | flops 910000000 | bytes 150000 | tf_op jit(solution)/shard_map/pairs/pallas_call | solution.py:294
  53.4 1.5 %hand_over.1 = (f32[16,768]{1,0:T(8,128)}, f32[16,768]{1,0:T(8,128)}, f32[3]{0:T(128)}) custom-call(f32[16,768]{1,0:T(8,128)} %get-tuple-element.6.a, f32[16,768]{1,0:T(8,128)} %get-tuple-element.7.b, f32[1,128]{1,0:T(1,128)} %get-tuple-element.8.c), custom_call_target="tpu_custom_call" | custom-call | tf_op jit(solution)/shard_map/hand_over/pallas_call | solution.py:327

commit v3 on v2

--- a/solution.py
+++ b/solution.py
@@ -25,7 +25,7 @@
 def kernel(
     pic_in, cap_in, heat, shift, g_img, g_txt, means,
     pic, cap, images, texts, sims, scaled, scaled_t, img_term, img_send, txt_send, txt_own,
-    from_x, to_y, from_y, from_c, to_z, from_z, to_far, part, sum_in,
+    from_x, to_y, from_y, from_y4, from_c, to_z, from_z, to_far, part, sum_in,
     s_in, s_gather, r_gather, s_scatter, r_scatter, s_sum, r_sum,
 ):
     img, txt = lax.axis_index("img"), lax.axis_index("txt")
@@ -84,8 +84,8 @@
 
     send = sender(s_gather, r_gather)
     own_t, own_i = slots(texts, 0), slots(images, 0)
-    over_z = {d: send(own_t, slots(texts, SLOT[d]), at(dz=-d)) for d in (4, 8, 3, 9, 2, 10, 1, 11)}
-    over_y = {k: send(own_i, slots(images, 4 * k), at(dy=-DY[k])) for k in range(1, 8)}
+    over_z = {d: send(own_t, slots(texts, SLOT[d]), at(dz=-d)) for d in (4, 8)}
+    over_y = {k: send(own_i, slots(images, 4 * k), at(dy=-DY[k])) for k in range(1, 7)}
     over_x, over_c = {}, []
 
     def forward_x(*ks):
@@ -100,6 +100,11 @@
 
     forward_x(0)
     forward_c(0)
+    forward_x(1, 2)
+    for d in (3, 9, 2, 10, 1, 11):
+        over_z[d] = send(own_t, slots(texts, SLOT[d]), at(dz=-d))
+    wait(over_x[0])
+    over_x[7] = [send(slots(images, 0, 4), slots(images, 28, 4), at(dy=-4))]
     wait([over_z[4], over_z[8]])
     six = SLOT[6] * B
     late = [
@@ -108,11 +113,11 @@
         send(slots(texts, SLOT[4]), slots(texts, SLOT[5]), at(dz=-1)),
         send(slots(texts, SLOT[8]), slots(texts, SLOT[7]), at(dz=1)),
     ]
-    forward_x(1, 2, 3, 4)
+    forward_x(3, 4)
     forward_c(4, 8)
     wait([over_z[d] for d in (1, 11, 2, 10)])
     forward_c(1, 11, 2, 10)
-    forward_x(5, 6, 7)
+    forward_x(5, 6)
     wait([over_z[d] for d in (3, 9)])
     forward_c(3, 9)
     wait(late)
@@ -163,7 +168,8 @@
     for p, (a, b) in enumerate(PARTS):
         ks = (range(0, 5), range(5, 8))[p]
         for k in ks:
-            wait(over_x[k])
+            if k:
+                wait(over_x[k])
         sims[a:b, :] = lax.dot_general(images[a:b, :], texts[...], nt, preferred_element_type=jnp.float32)
         sums = lax.fori_loop(a // step, b // step, pairs, sums)
         if p:
@@ -190,7 +196,13 @@
                     value = value + sum_in[i]
                 return value
 
-            sum_c = spread(0, total, [at(dc=1)])
+            plane = [at(dx, dy) for dy in DY[::-1] for dx in (2, 1, 3, 0) if dx or dy]
+            sum_p = spread(0, total, plane)
+            scaled_t[...] = scaled[...].T
+            txt_send[...] = jnp.dot(scaled_t[CR:, :], images[...], preferred_element_type=jnp.float32).astype(jnp.bfloat16)
+            cut = SLOT[4]
+            back_c = [send(slots(txt_send, i, n), slots(from_c, i, n), at(dc=1)) for i, n in ((cut, NZ - cut), (0, cut))]
+            txt_own[...] = jnp.dot(scaled_t[0:CR, :], images[...], preferred_element_type=jnp.float32)
         term = jnp.dot(scaled[a:b, :], texts[...], preferred_element_type=jnp.float32)
         img_term[a:b, :] = term
         img_send[a:b, :] = term.astype(jnp.bfloat16)
@@ -198,29 +210,31 @@
         for k in ks:
             back_x[k] = [send(slots(img_send, 4 * k + dx), slots(from_x, 4 * k + dx), at(dx=dx)) for dx in DX]
 
-    send_x(7, 6, 5)
-    scaled_t[...] = scaled[...].T
-    txt_send[...] = jnp.dot(scaled_t[CR:, :], images[...], preferred_element_type=jnp.float32).astype(jnp.bfloat16)
-    back_c = send(txt_send, from_c, at(dc=1))
-    txt_own[...] = jnp.dot(scaled_t[0:CR, :], images[...], preferred_element_type=jnp.float32)
-    total = collect(total, sum_c)
-    plane = [at(dx, dy) for dy in DY[::-1] for dx in (2, 1, 3, 0) if dx or dy]
-    sum_p = spread(1, total, plane)
-
-    back_c.wait_recv()
-    txt_own[...] = txt_own[...] + from_c[...].astype(jnp.float32)
-    to_z[...] = txt_own[...].astype(jnp.bfloat16)
+    back_y4 = send(slots(img_send, 28, 4), from_y4, at(dy=4))
+    send_x(6, 5, 4, 3, 2, 1)
+
+    def add_c(first, last):
+        value = txt_own[first * B:last * B, :] + from_c[first * B:last * B, :].astype(jnp.float32)
+        txt_own[first * B:last * B, :] = value
+        to_z[first * B:last * B, :] = value.astype(jnp.bfloat16)
+
+    back_c[0].wait_recv()
+    add_c(cut, NZ)
     relay = [
         send(to_z.at[pl.ds(six, B), pl.ds(0, HALF)], from_z.at[pl.ds(six, B), pl.ds(0, HALF)], at(dz=2)),
         send(to_z.at[pl.ds(six, B), pl.ds(HALF, HALF)], from_z.at[pl.ds(six, B), pl.ds(HALF, HALF)], at(dz=-2)),
         send(slots(to_z, SLOT[5]), slots(from_z, SLOT[5]), at(dz=1)),
         send(slots(to_z, SLOT[7]), slots(from_z, SLOT[7]), at(dz=-1)),
     ]
-    back_z = {d: send(slots(to_z, SLOT[d]), slots(from_z, SLOT[d]), at(dz=d)) for d in (3, 9, 2, 10, 1, 11)}
-    for k in (7, 6, 5):
-        for copy in back_x[k]:
-            copy.wait_send()
-    send_x(4, 3, 2, 1, 0)
+    back_c[1].wait_recv()
+    add_c(0, cut)
+    back_z = {}
+
+    def send_z(*ds):
+        for d in ds:
+            back_z[d] = send(slots(to_z, SLOT[d]), slots(from_z, SLOT[d]), at(dz=d))
+
+    send_z(2, 10, 1, 11)
 
     wait(relay)
 
@@ -233,6 +247,15 @@
     to_far[B:, :] = (piece(txt_own, 8) + piece(from_z, 7) + jnp.where(side, 0.0, both)).astype(jnp.bfloat16)
     for i, d in enumerate((4, 8)):
         back_z[d] = send(slots(to_far, i), slots(from_z, SLOT[d]), at(dz=d))
+    send_z(3, 9)
+    total = collect(total, sum_p)
+    column = [at(dz=d, dc=other) for d in DZ[::-1] for other in (0, 1) if d or other]
+    sum_z = spread(1, total, column)
+    back_y4.wait_recv()
+    near_y = img_term[0:4 * B, :] + from_y4[...].astype(jnp.float32)
+    img_term[0:4 * B, :] = near_y
+    img_send[0:4 * B, :] = near_y.astype(jnp.bfloat16)
+    send_x(0)
     back_y = []
 
     def image_sum(k):
@@ -248,10 +271,7 @@
             to_y[(k - 1) * B:k * B, :] = image_sum(k).astype(jnp.bfloat16)
             back_y.append(send(slots(to_y, k - 1), slots(from_y, k - 1), at(dy=DY[k])))
 
-    total = collect(total, sum_p)
-    sum_z = spread(2, total, [at(dz=d) for d in DZ[:0:-1]])
-    send_y(7, 6, 5)
-    send_y(4, 3, 2, 1)
+    send_y(6, 5, 4, 3, 2, 1)
     img_dir = image_sum(0)
 
     def back_norm(unit, direction, norm):
@@ -264,15 +284,13 @@
         txt_dir = txt_dir + piece(from_z, d)
     g_txt[...] = back_norm(txt_unit, txt_dir, txt_norm)
     wait(back_y)
-    for k in range(1, 8):
+    for k in range(1, 7):
         img_dir = img_dir + from_y[(k - 1) * B:k * B, :].astype(jnp.float32)
     g_img[...] = back_norm(img_unit, img_dir, img_norm)
     total = collect(total, sum_z)
     means[...] = total * jnp.where(lane == 2, temp[:, 0:128], 1.0) * (1.0 / (COUNT * COUNT))
-    early = {id(copy) for k in (7, 6, 5) for copy in back_x[k]}
     for copy in sends:
-        if id(copy) not in early:
-            copy.wait_send()
+        copy.wait_send()
 
 
 def hand_over(a, b, c, a_out, b_out, c_out):
@@ -311,13 +329,14 @@
             pltpu.VMEM((IMG, E), bf16),
             pltpu.VMEM((7 * B, E), bf16),
             pltpu.VMEM((7 * B, E), bf16),
+            pltpu.VMEM((4 * B, E), bf16),
             pltpu.VMEM((CR, E), bf16),
             pltpu.VMEM((CR, E), bf16),
             pltpu.VMEM((CR, E), bf16),
             pltpu.VMEM((2 * B, E), bf16),
-            pltpu.VMEM((3, 1, 128), f32),
-            pltpu.VMEM((43, 1, 128), f32),
-            dma((2,)), dma((48,)), dma((48,)), dma((44,)), dma((44,)), dma((43,)), dma((43,)),
+            pltpu.VMEM((2, 1, 128), f32),
+            pltpu.VMEM((54, 1, 128), f32),
+            dma((2,)), dma((48,)), dma((48,)), dma((44,)), dma((44,)), dma((54,)), dma((54,)),
         ],
         compiler_params=pltpu.CompilerParams(
             collective_id=0, has_side_effects=True, vmem_limit_bytes=62 * 1024 * 1024),

time: 55.1 us -> 54.7 us (level)
  no operation moved by 1% of the time
where the time goes in v3:
time: 54.7 us; the launch traced here: 54.4 us
  Pallas kernels  52.5 us (96%)
  between operations  1.93 us (4%)
    pallas_call x1, Pallas kernels, per_device(): pl.pallas_call(kernel, out_shape=results_shape, in_specs=[hbm, hbm, smem,...  51 us
    pallas_call x1, Pallas kernels, per_device(): pl.pallas_call(hand_over, out_shape=(*results_shape[:2], jax.ShapeDtypeSt...  1.48 us

profile of v3, /device:TPU:1, one launch (start us, length us, event | category | flops | bytes accessed | tf_op | source)
XLA Modules:
  0.0 54.4 jit_solution(9321856933329645635)
XLA Ops:
  1.9 51.0 %pairs.1 = (f32[16,768]{1,0:T(8,128)}, f32[16,768]{1,0:T(8,128)}, f32[1,128]{1,0:T(1,128)}) custom-call(bf16[16,768]{1,0:T(8,128)(2,1)} %pic_in.1, bf16[16,768]{1,0:T(8,128)(2,1)} %cap_in.1, f32[1]{0:T(128)} %bitcast.2.heat, f32[1]{0:T(128)} %bitcast.3.shift), custom_call_target="tpu_custom_call" | custom-call | flops 910000000 | bytes 150000 | tf_op jit(solution)/shard_map/pairs/pallas_call | solution.py:312
  52.9 1.5 %hand_over.1 = (f32[16,768]{1,0:T(8,128)}, f32[16,768]{1,0:T(8,128)}, f32[3]{0:T(128)}) custom-call(f32[16,768]{1,0:T(8,128)} %get-tuple-element.6.a, f32[16,768]{1,0:T(8,128)} %get-tuple-element.7.b, f32[1,128]{1,0:T(1,128)} %get-tuple-element.8.c), custom_call_target="tpu_custom_call" | custom-call | tf_op jit(solution)/shard_map/hand_over/pallas_call | solution.py:346

commit v4 on v3

--- a/solution.py
+++ b/solution.py
@@ -236,6 +236,9 @@
 
     send_z(2, 10, 1, 11)
 
+    total = collect(total, sum_p)
+    column = [at(dz=d, dc=other) for d in DZ[::-1] for other in (0, 1) if d or other]
+    sum_z = spread(1, total, column)
     wait(relay)
 
     def piece(ref, d):
@@ -248,9 +251,6 @@
     for i, d in enumerate((4, 8)):
         back_z[d] = send(slots(to_far, i), slots(from_z, SLOT[d]), at(dz=d))
     send_z(3, 9)
-    total = collect(total, sum_p)
-    column = [at(dz=d, dc=other) for d in DZ[::-1] for other in (0, 1) if d or other]
-    sum_z = spread(1, total, column)
     back_y4.wait_recv()
     near_y = img_term[0:4 * B, :] + from_y4[...].astype(jnp.float32)
     img_term[0:4 * B, :] = near_y

time: 54.7 us -> 53 us (0.969)
  Pallas kernels: 52.5 us -> 50.8 us
    pallas_call x1, Pallas kernels: 51 us -> 49.3 us  [per_device(): pl.pallas_call(kernel, out_shape=results_shape, in_specs=[hbm, hbm, smem,...]
where the time goes in v4:
time: 53 us; the launch traced here: 52.7 us
  Pallas kernels  50.8 us (96%)
  between operations  1.93 us (4%)
    pallas_call x1, Pallas kernels, per_device(): pl.pallas_call(kernel, out_shape=results_shape, in_specs=[hbm, hbm, smem,...  49.3 us
    pallas_call x1, Pallas kernels, per_device(): pl.pallas_call(hand_over, out_shape=(*results_shape[:2], jax.ShapeDtypeSt...  1.48 us

profile of v4, /device:TPU:1, one launch (start us, length us, event | category | flops | bytes accessed | tf_op | source)
XLA Modules:
  0.0 52.7 jit_solution(4374802687741962875)
XLA Ops:
  1.9 49.3 %pairs.1 = (f32[16,768]{1,0:T(8,128)}, f32[16,768]{1,0:T(8,128)}, f32[1,128]{1,0:T(1,128)}) custom-call(bf16[16,768]{1,0:T(8,128)(2,1)} %pic_in.1, bf16[16,768]{1,0:T(8,128)(2,1)} %cap_in.1, f32[1]{0:T(128)} %bitcast.2.heat, f32[1]{0:T(128)} %bitcast.3.shift), custom_call_target="tpu_custom_call" | custom-call | flops 910000000 | bytes 150000 | tf_op jit(solution)/shard_map/pairs/pallas_call | solution.py:312
  51.3 1.5 %hand_over.1 = (f32[16,768]{1,0:T(8,128)}, f32[16,768]{1,0:T(8,128)}, f32[3]{0:T(128)}) custom-call(f32[16,768]{1,0:T(8,128)} %get-tuple-element.6.a, f32[16,768]{1,0:T(8,128)} %get-tuple-element.7.b, f32[1,128]{1,0:T(1,128)} %get-tuple-element.8.c), custom_call_target="tpu_custom_call" | custom-call | tf_op jit(solution)/shard_map/hand_over/pallas_call | solution.py:346

commit v5 on v4

--- a/solution.py
+++ b/solution.py
@@ -211,7 +211,7 @@
             back_x[k] = [send(slots(img_send, 4 * k + dx), slots(from_x, 4 * k + dx), at(dx=dx)) for dx in DX]
 
     back_y4 = send(slots(img_send, 28, 4), from_y4, at(dy=4))
-    send_x(6, 5, 4, 3, 2, 1)
+    send_x(6, 5, 4)
 
     def add_c(first, last):
         value = txt_own[first * B:last * B, :] + from_c[first * B:last * B, :].astype(jnp.float32)
@@ -235,6 +235,7 @@
             back_z[d] = send(slots(to_z, SLOT[d]), slots(from_z, SLOT[d]), at(dz=d))
 
     send_z(2, 10, 1, 11)
+    send_x(3, 2, 1)
 
     total = collect(total, sum_p)
     column = [at(dz=d, dc=other) for d in DZ[::-1] for other in (0, 1) if d or other]

time: 53 us -> 53 us (level)
  no operation moved by 1% of the time
where the time goes in v5:
time: 53 us; the launch traced here: 52.7 us
  Pallas kernels  50.8 us (96%)
  between operations  1.93 us (4%)
    pallas_call x1, Pallas kernels, per_device(): pl.pallas_call(kernel, out_shape=results_shape, in_specs=[hbm, hbm, smem,...  49.3 us
    pallas_call x1, Pallas kernels, per_device(): pl.pallas_call(hand_over, out_shape=(*results_shape[:2], jax.ShapeDtypeSt...  1.48 us

profile of v5, /device:TPU:1, one launch (start us, length us, event | category | flops | bytes accessed | tf_op | source)
XLA Modules:
  0.0 52.7 jit_solution(6507764025071278318)
XLA Ops:
  1.9 49.3 %pairs.1 = (f32[16,768]{1,0:T(8,128)}, f32[16,768]{1,0:T(8,128)}, f32[1,128]{1,0:T(1,128)}) custom-call(bf16[16,768]{1,0:T(8,128)(2,1)} %pic_in.1, bf16[16,768]{1,0:T(8,128)(2,1)} %cap_in.1, f32[1]{0:T(128)} %bitcast.2.heat, f32[1]{0:T(128)} %bitcast.3.shift), custom_call_target="tpu_custom_call" | custom-call | flops 910000000 | bytes 150000 | tf_op jit(solution)/shard_map/pairs/pallas_call | solution.py:313
  51.3 1.5 %hand_over.1 = (f32[16,768]{1,0:T(8,128)}, f32[16,768]{1,0:T(8,128)}, f32[3]{0:T(128)}) custom-call(f32[16,768]{1,0:T(8,128)} %get-tuple-element.6.a, f32[16,768]{1,0:T(8,128)} %get-tuple-element.7.b, f32[1,128]{1,0:T(1,128)} %get-tuple-element.8.c), custom_call_target="tpu_custom_call" | custom-call | tf_op jit(solution)/shard_map/hand_over/pallas_call | solution.py:347
